TPU v7x, 32 devices: a whole 2x2x4 slice. The times are simulated.
32 devices in a mesh: parts: 2 (over y), dp: 4 (over z), tensor: 4 (over x, core).
Axes of the slice: x: 2, y: 2, z: 4, core: 2. Of those that a mesh axis runs over, the one named last changes fastest.
Arguments:
- activations: bfloat16 [4096, 8192], P(('parts', 'dp', 'tensor')), parts along dimension 0, may hold values from -6 to 6
- query_cotangent: bfloat16 [4096, 8192], P(('parts', 'dp'), 'tensor'), parts along dimension 0, may hold values from -6 to 6
- value_cotangent: bfloat16 [4096, 1024], P(('parts', 'dp'), 'tensor'), parts along dimension 0, may hold values from -6 to 6
- query_matrix: bfloat16 [8192, 8192], P(None, 'tensor'), may hold values from -0.0625 to 0.0625
- value_matrix: bfloat16 [8192, 1024], P(None, 'tensor'), may hold values from -0.0625 to 0.0625
- block_tenant: int32 [64], P(('parts', 'dp')), parts along dimension 0, may hold values from 0 to 7
- owner_slot: int32 [16], P('parts'), parts along dimension 0, may hold values from 0 to 7, as said below
- slot_step: int32 [16], P(('parts', 'dp')), parts along dimension 0, may hold values from 1 to 2000
- down_state: float32 [16, 3, 2, 32, 8192], P(('parts', 'dp'), None, None, None, 'tensor'), parts along dimension 0, as said below
- query_state: float32 [16, 3, 32, 8192], P(('parts', 'dp'), None, None, 'tensor'), parts along dimension 0, as said below
- value_state: float32 [16, 3, 32, 1024], P(('parts', 'dp'), None, None, 'tensor'), parts along dimension 0, as said below
- serve_tenant: int32 [32], P('parts'), parts along dimension 0, may hold values from 0 to 7, as said below
Outputs:
- input_cotangent: bfloat16 [4096, 8192], P(('parts', 'dp', 'tensor')), parts along dimension 0
- new_down: float32 [16, 2, 2, 32, 8192], P(('parts', 'dp'), None, None, None, 'tensor'), parts along dimension 0
- new_down_master: float32 [16, 2, 32, 8192], P(('parts', 'dp'), None, None, 'tensor'), parts along dimension 0
- new_query: float32 [16, 3, 32, 8192], P(('parts', 'dp'), None, None, 'tensor'), parts along dimension 0
- new_value: float32 [16, 3, 32, 1024], P(('parts', 'dp'), None, None, 'tensor'), parts along dimension 0
- served_down: bfloat16 [32, 2, 32, 8192], P(('parts', 'dp'), None, None, 'tensor'), parts along dimension 0
- served_query: bfloat16 [32, 32, 8192], P(('parts', 'dp'), None, 'tensor'), parts along dimension 0
- served_value: bfloat16 [32, 32, 1024], P(('parts', 'dp'), None, 'tensor'), parts along dimension 0
There are 2 independent parts, one for each index of `parts`. A program takes and returns all parts, laid end to end along the dimension named above; an argument that names none is the same for every part. Nothing has to cross between parts.
Inputs may be any that keep to these rules, and one draw needn't show every extreme that they name: `owner_slot`: each row number appears once; the tenants of rows s with equal s // 2 share an owner. `serve_tenant`: the 4 slots of one replica (slots 4 * r to 4 * r + 3) name tenants whose values owner_slot // 2 all differ. `down_state`: entry 2 along dimension 1 (second moments) lies in 0.1 to 10. `query_state`: entry 2 along dimension 1 (second moments) lies in 0.01 to 1. `value_state`: entry 2 along dimension 1 (second moments) lies in 0.01 to 1.
All inputs are finite; a program needn't handle non-finite values.
Results may differ from a plain program's by a relative error of at most 0.015.
Values may be sent and summed in bfloat16 or wider, within the bound.
A program may use at most 192 MiB of HBM per device.

v0:
```python
import functools
import math

import jax
import jax.numpy as jnp
from jax import lax
from jax.experimental import pallas as pl
from jax.experimental.pallas import tpu as pltpu
from jax.sharding import PartitionSpec as P

ADAPTER_SCALE = 0.25
BETA_ONE = 0.9
BETA_TWO = 0.999
LEARN_RATE = 0.02
WEIGHT_DECAY = 0.01
ADAM_EPSILON = 1e-08

F32 = jnp.float32
BF16 = jnp.bfloat16


def dot(a, b, ca, cb):
    return lax.dot_general(a, b, (((ca,), (cb,)), ((), ())), preferred_element_type=F32)


def adam_parts(packed_state, gradient, counts):
    master = packed_state[:, 0]
    first = BETA_ONE * packed_state[:, 1] + (1.0 - BETA_ONE) * gradient
    second = BETA_TWO * packed_state[:, 2] + (1.0 - BETA_TWO) * gradient * gradient
    shaped = counts.astype(F32).reshape((-1,) + (1,) * (gradient.ndim - 1))
    fix_one = 1.0 - jnp.exp(shaped * math.log(BETA_ONE))
    fix_two = 1.0 - jnp.exp(shaped * math.log(BETA_TWO))
    master = master - LEARN_RATE * (
        first / fix_one / (jnp.sqrt(second / fix_two) + ADAM_EPSILON) + WEIGHT_DECAY * master
    )
    return master, first, second


MESH = pl.DeviceIdType.MESH
ANY = pl.BlockSpec(memory_space=pl.ANY)
VMEM = pl.BlockSpec(memory_space=pltpu.VMEM)
DMA = pltpu.SemaphoreType.DMA


def meet(sizes):
    barrier = pltpu.get_barrier_semaphore()
    for axis, n in sizes.items():
        me = lax.axis_index(axis)
        for s in range(1, n):
            pl.semaphore_signal(
                barrier, inc=1, device_id={axis: lax.rem(me + s, n)}, device_id_type=MESH
            )
    pl.semaphore_wait(barrier, sum(n - 1 for n in sizes.values()))


def to_peer(axis, n, s, source, target, send, recv):
    me = lax.axis_index(axis)
    peer = lax.rem(me + s, n)
    return pltpu.make_async_remote_copy(
        src_ref=source(peer),
        dst_ref=target(me),
        send_sem=send.at[s],
        recv_sem=recv.at[s],
        device_id={axis: peer},
        device_id_type=MESH,
    )


def from_peer(axis, n, s, source, target, send, recv):
    me = lax.axis_index(axis)
    return pltpu.make_async_remote_copy(
        src_ref=source(lax.rem(me + s, n)),
        dst_ref=target(lax.rem(me + n - s, n)),
        send_sem=send.at[s],
        recv_sem=recv.at[s],
        device_id={axis: lax.rem(me + s, n)},
        device_id_type=MESH,
    )


def launch(jobs):
    for axis, n, source, target, send, recv in jobs:
        for s in range(1, n):
            to_peer(axis, n, s, source, target, send, recv).start()
    for axis, n, source, target, send, recv in jobs:
        me = lax.axis_index(axis)
        pltpu.make_async_copy(source(me), target(me), send.at[0]).start()


def finish(jobs):
    for axis, n, source, target, send, recv in jobs:
        me = lax.axis_index(axis)
        pltpu.make_async_copy(source(me), target(me), send.at[0]).wait()
        for s in range(1, n):
            to_peer(axis, n, s, source, target, send, recv).wait_send()
            from_peer(axis, n, s, source, target, send, recv).wait_recv()


def swap_kernel(sizes, axes, *refs):
    k = len(axes)
    sources, results, sems = refs[:k], refs[k : 2 * k], refs[2 * k :]
    meet(sizes)
    jobs = []
    for i, axis in enumerate(axes):
        source, result = sources[i], results[i]
        jobs.append(
            (
                axis,
                sizes[axis],
                lambda p, r=source: r.at[p],
                lambda p, r=result: r.at[p],
                sems[2 * i],
                sems[2 * i + 1],
            )
        )
    launch(jobs)
    finish(jobs)


def swap(arrays, axes, sizes, ident):
    sizes = {a: sizes[a] for a in sizes if a in axes}
    return pl.pallas_call(
        functools.partial(swap_kernel, sizes, axes),
        out_shape=[jax.ShapeDtypeStruct(a.shape, a.dtype) for a in arrays],
        in_specs=[ANY] * len(arrays),
        out_specs=[ANY] * len(arrays),
        scratch_shapes=[DMA((sizes[a],)) for a in axes for _ in range(2)],
        compiler_params=pltpu.CompilerParams(collective_id=ident, has_side_effects=True),
        name="swap_%d" % ident,
    )(*arrays)


def low_kernel(n, part, out, came, send, recv):
    meet({"tensor": n})
    for s in range(1, n):
        to_peer(
            "tensor", n, s, lambda p: part, lambda p: came.at[p], send, recv
        ).start()
    me = lax.axis_index("tensor")
    came[me] = part[...]
    for s in range(1, n):
        to_peer("tensor", n, s, lambda p: part, lambda p: came.at[p], send, recv).wait_send()
        from_peer("tensor", n, s, lambda p: part, lambda p: came.at[p], send, recv).wait_recv()
    total = came[0].astype(F32)
    for p in range(1, n):
        total = total + came[p].astype(F32)
    out[...] = total.astype(BF16)


def add_everywhere(part, n):
    return pl.pallas_call(
        functools.partial(low_kernel, n),
        out_shape=jax.ShapeDtypeStruct(part.shape, BF16),
        in_specs=[VMEM],
        out_specs=VMEM,
        scratch_shapes=[pltpu.VMEM((n,) + part.shape, BF16), DMA((n,)), DMA((n,))],
        compiler_params=pltpu.CompilerParams(collective_id=1, has_side_effects=True),
        name="low_sums",
    )(part)


def main_kernel(
    groups,
    n,
    lhs_q,
    lhs_v,
    query_matrix,
    value_matrix,
    activations,
    own_wide,
    own_value,
    out,
    feats,
    all_wide,
    all_value,
    weight,
    weight_v,
    part,
    near,
    mine,
    far,
    w_sem,
    wv_sem,
    near_send,
    near_recv,
    far_send,
    far_recv,
    feat_send,
    feat_recv,
    wide_send,
    wide_recv,
    value_send,
    value_recv,
):
    steps, cols = part.shape[0], part.shape[2]
    half = part.shape[1] // 2
    chips = n // 2
    rows = half // chips
    width = lhs_q.shape[1]
    t = lax.axis_index("tensor")
    chip, core = t // 2, lax.rem(t, 2)

    def load(j):
        slot = lax.rem(j, 2)
        at = pl.ds(pl.multiple_of(j * cols, cols), cols)
        return (
            pltpu.make_async_copy(query_matrix.at[at], weight.at[slot], w_sem.at[slot]),
            pltpu.make_async_copy(value_matrix.at[at], weight_v.at[slot], wv_sem.at[slot]),
        )

    for c in load(0):
        c.start()
    meet({"dp": groups, "tensor": n})
    jobs = [
        (
            "tensor",
            n,
            lambda p: activations.at[:, pl.ds(pl.multiple_of(p * width, width), width)],
            lambda p: feats.at[p],
            feat_send,
            feat_recv,
        ),
        ("dp", groups, lambda p: own_value, lambda p: all_value.at[p], value_send, value_recv),
        ("dp", groups, lambda p: own_wide, lambda p: all_wide.at[p], wide_send, wide_recv),
    ]
    launch(jobs)

    def near_copy(j):
        return pltpu.make_async_remote_copy(
            src_ref=part.at[j, pl.ds(0, half)],
            dst_ref=near.at[j],
            send_sem=near_send.at[j],
            recv_sem=near_recv.at[j],
            device_id={"tensor": 2 * chip + 1 - core},
            device_id_type=MESH,
        )

    def far_copy(k, j):
        return pltpu.make_async_remote_copy(
            src_ref=mine.at[k, j],
            dst_ref=far.at[k, j],
            send_sem=far_send.at[k, j],
            recv_sem=far_recv.at[k, j],
            device_id={"tensor": 2 * lax.rem(chip + k, chips) + core},
            device_id_type=MESH,
        )

    def join(j):
        near_copy(j).wait()
        for k in range(chips):
            here = pl.ds(half + k * rows, rows)
            there = pl.ds(k * rows, rows)
            both = part[j, here].astype(F32) + near[j, there].astype(F32)
            mine[k, j] = both.astype(BF16)
        for k in range(1, chips):
            far_copy(k, j).start()

    def step(j, carry):
        @pl.when(j + 1 < steps)
        def _():
            for c in load(j + 1):
                c.start()

        for c in load(j):
            c.wait()
        slot = lax.rem(j, 2)
        p = dot(lhs_q[...], weight[slot], 1, 1) + dot(lhs_v[...], weight_v[slot], 1, 1)
        part[j] = p.astype(BF16)
        near_copy(j).start()

        @pl.when(j >= 1)
        def _():
            join(j - 1)

        return carry

    lax.fori_loop(0, steps, step, 0)
    join(steps - 1)

    def last(j, carry):
        total = mine[0, j].astype(F32)
        for k in range(1, chips):
            far_copy(k, j).wait()
            total = total + far[k, j].astype(F32)
        out[j] = total.astype(BF16)
        return carry

    lax.fori_loop(0, steps, last, 0)
    finish(jobs)


def main_call(groups, n, lhs_q, lhs_v, query_matrix, value_matrix, activations, own_wide, own_value):
    tokens, width = lhs_q.shape
    rows = activations.shape[0]
    cols = 512
    steps = query_matrix.shape[0] // cols
    chips = n // 2
    half = tokens // 2
    s = jax.ShapeDtypeStruct
    return pl.pallas_call(
        functools.partial(main_kernel, groups, n),
        out_shape=[
            s((steps, rows, cols), BF16),
            s((n, rows, width), BF16),
            s((groups,) + own_wide.shape, BF16),
            s((groups,) + own_value.shape, BF16),
        ],
        in_specs=[VMEM, VMEM] + [ANY] * 5,
        out_specs=[VMEM, ANY, ANY, ANY],
        scratch_shapes=[
            pltpu.VMEM((2, cols, width), BF16),
            pltpu.VMEM((2, cols, lhs_v.shape[1]), BF16),
            pltpu.VMEM((steps, tokens, cols), BF16),
            pltpu.VMEM((steps, half, cols), BF16),
            pltpu.VMEM((chips, steps, rows, cols), BF16),
            pltpu.VMEM((chips, steps, rows, cols), BF16),
            DMA((2,)),
            DMA((2,)),
            DMA((steps,)),
            DMA((steps,)),
            DMA((chips, steps)),
            DMA((chips, steps)),
            DMA((n,)),
            DMA((n,)),
            DMA((groups,)),
            DMA((groups,)),
            DMA((groups,)),
            DMA((groups,)),
        ],
        compiler_params=pltpu.CompilerParams(
            collective_id=0, has_side_effects=True, vmem_limit_bytes=48 * 1024 * 1024
        ),
        name="frozen_and_gathers",
    )(lhs_q, lhs_v, query_matrix, value_matrix, activations, own_wide, own_value)


def body(
    activations,
    query_cotangent,
    value_cotangent,
    query_matrix,
    value_matrix,
    block_tenant,
    owner_slot,
    slot_step,
    down_state,
    query_state,
    value_state,
    serve_tenant,
):
    G = lax.axis_size("dp")
    T = lax.axis_size("tensor")
    sizes = {"dp": G, "tensor": T}
    g = lax.axis_index("dp")
    t = lax.axis_index("tensor")
    chips = T // 2
    core, chip = t % 2, t // 2
    tokens, width = query_cotangent.shape
    value_here = value_cotangent.shape[1]
    rows = activations.shape[0]
    owned, rank = query_state.shape[0], query_state.shape[2]
    slots = owned * G
    block_len = tokens // block_tenant.shape[0]
    served_here = serve_tenant.shape[0] // G

    own_wide = jnp.concatenate(
        [query_state[:, 0].reshape(owned * rank, width), down_state[:, 0].reshape(-1, width)], axis=0
    ).astype(BF16)
    own_value = value_state[:, 0].astype(BF16).reshape(owned * rank, value_here)

    def ordered(a):
        cut = [
            lax.dynamic_slice_in_dim(a, (2 * ((chip + k) % chips) + c) * rows, rows, 0)
            for c in (1 - core, core)
            for k in range(chips)
        ]
        return jnp.concatenate(cut, axis=0)

    frozen, feats, all_wide, all_value = main_call(
        G,
        T,
        ordered(query_cotangent),
        ordered(value_cotangent),
        query_matrix,
        value_matrix,
        activations,
        own_wide,
        own_value,
    )
    feats = feats.reshape(tokens, width)
    work_query = all_wide[:, : owned * rank].reshape(slots * rank, width)
    work_down = all_wide[:, owned * rank :].reshape(slots * 2 * rank, width)
    work_value = all_value.reshape(slots * rank, value_here)

    position = jnp.repeat(owner_slot[block_tenant], block_len)
    mask = jnp.arange(slots, dtype=jnp.int32)[:, None, None] == position[None, None, :]

    def pick(product):
        p = product.reshape(slots, -1, tokens)
        return jnp.sum(jnp.where(mask, p, 0.0), axis=0)

    def spread(low):
        return jnp.where(mask, low[None], jnp.zeros((), BF16)).reshape(-1, tokens)

    part = jnp.concatenate(
        [
            pick(dot(work_query, query_cotangent, 1, 1)),
            pick(dot(work_value, value_cotangent, 1, 1)),
            pick(dot(work_down, feats, 1, 1)),
        ],
        axis=0,
    ).astype(BF16)
    low = add_everywhere(part, T)
    low_u, low_h = low[: 2 * rank], low[2 * rank :]
    low_u_at = spread(low_u)

    down_part = (ADAPTER_SCALE * dot(low_u_at, feats, 1, 0)).astype(BF16)
    query_part = (ADAPTER_SCALE * dot(spread(low_h[:rank]), query_cotangent, 1, 0)).astype(BF16)
    value_part = (ADAPTER_SCALE * dot(spread(low_h[rank:]), value_cotangent, 1, 0)).astype(BF16)
    lora = (ADAPTER_SCALE * dot(low_u_at, work_down, 0, 0)).astype(BF16)

    down_came, query_came, value_came, lora_came = swap(
        [
            down_part.reshape(G, owned * 2 * rank, width),
            query_part.reshape(G, owned * rank, width),
            value_part.reshape(G, owned * rank, value_here),
            lora.reshape(T, rows, width),
        ],
        ("dp", "dp", "dp", "tensor"),
        sizes,
        2,
    )
    down_grad = jnp.sum(down_came.astype(F32), axis=0).reshape(owned, 2, rank, width)
    query_grad = jnp.sum(query_came.astype(F32), axis=0).reshape(owned, rank, width)
    value_grad = jnp.sum(value_came.astype(F32), axis=0).reshape(owned, rank, value_here)

    d_master, d_first, d_second = adam_parts(down_state, down_grad, slot_step)
    q_master, q_first, q_second = adam_parts(query_state, query_grad, slot_step)
    v_master, v_first, v_second = adam_parts(value_state, value_grad, slot_step)

    serve_rows = owner_slot[serve_tenant].reshape(G, served_here)
    row = jnp.sum(jnp.where(serve_rows // owned == g, serve_rows % owned, 0), axis=1)

    def wanted(master):
        fresh = master.astype(BF16)[None]
        pick_row = row.reshape((-1,) + (1,) * (fresh.ndim - 2))
        out = fresh[:, 0]
        for r in range(1, owned):
            out = jnp.where(pick_row == r, fresh[:, r], out)
        return out

    down_new, query_new, value_new = swap(
        [wanted(d_master), wanted(q_master), wanted(v_master)], ("dp",) * 3, sizes, 3
    )
    owner = lax.dynamic_index_in_dim(serve_rows, g, 0, False) // owned

    def served(came):
        return jnp.stack(
            [lax.dynamic_index_in_dim(came, owner[q], 0, False) for q in range(served_here)]
        )

    lora_cols = jnp.swapaxes(lora_came, 0, 1).reshape(rows, T * width)
    base = jnp.swapaxes(frozen, 0, 1).reshape(rows, T * width)
    input_cotangent = (base.astype(F32) + lora_cols.astype(F32)).astype(BF16)

    return (
        input_cotangent,
        jnp.stack([d_first, d_second], axis=1),
        d_master,
        jnp.stack([q_master, q_first, q_second], axis=1),
        jnp.stack([v_master, v_first, v_second], axis=1),
        served(down_new),
        served(query_new),
        served(value_new),
    )


def solution(mesh):
    in_specs = (
        P(("parts", "dp", "tensor"), None),
        P(("parts", "dp"), "tensor"),
        P(("parts", "dp"), "tensor"),
        P(None, "tensor"),
        P(None, "tensor"),
        P(("parts", "dp")),
        P("parts"),
        P(("parts", "dp")),
        P(("parts", "dp"), None, None, None, "tensor"),
        P(("parts", "dp"), None, None, "tensor"),
        P(("parts", "dp"), None, None, "tensor"),
        P("parts"),
    )
    out_specs = (
        P(("parts", "dp", "tensor"), None),
        P(("parts", "dp"), None, None, None, "tensor"),
        P(("parts", "dp"), None, None, "tensor"),
        P(("parts", "dp"), None, None, "tensor"),
        P(("parts", "dp"), None, None, "tensor"),
        P(("parts", "dp"), None, None, "tensor"),
        P(("parts", "dp"), None, "tensor"),
        P(("parts", "dp"), None, "tensor"),
    )
    return jax.shard_map(body, mesh=mesh, in_specs=in_specs, out_specs=out_specs, check_vma=False)
```

profile of v0, /device:TPU:0, one launch (start us, length us, event | category | flops | bytes accessed | tf_op | source)
XLA Modules:
  0.0 282.8 jit_solution(68446726570396391)
XLA Ops:
  2.1 1.8 constant_dynamic-slice_fusion.20
  3.9 1.6 pad_maximum_fusion.lhs_q
  5.5 1.3 bitcast_convert_fusion
  6.9 1.1 slice.169
  8.1 77.3 %frozen_and_gathers.1 = (bf16[16,128,512]{2,1,0:T(8,128)(2,1)S(1)}, bf16[4,128,2048]{2,1,0:T(8,128)(2,1)S(1)}, bf16[4,192,2048]{2,1,0:T(8,128)(2,1)}, bf16[4,64,256]{2,1,0:T(8,128)(2,1)S(1)}) custom-call(bf16[512,2048]{1,0:T(8,128)(2,1)} %pad_maximum_fusion.lhs_q, bf16[512,256]{1,0:T(8,128)(2,1)S(1)} %pad_maximum_fusion.6.lhs_v, ...), custom_call_target="tpu_custom_call" | custom-call | tf_op jit(solution)/shard_map/frozen_and_gathers/pallas_call | solution.py:300
  85.4 2.6 slice.90
  88.0 1.3 fusion.4
  89.7 1.5 slice.89
  92.7 8.4 %low_sums.1 = bf16[128,512]{1,0:T(8,128)(2,1)} custom-call(bf16[128,512]{1,0:T(8,128)(2,1)} %pad_maximum_fusion.8.part), custom_call_target="tpu_custom_call" | custom-call | tf_op jit(solution)/shard_map/low_sums/pallas_call | solution.py:151
  102.0 4.4 %multiply_convert_fusion.1 = bf16[512,2048]{1,0:T(8,128)(2,1)} fusion(bf16[512,512]{1,0:T(8,128)(2,1)S(1)} %bitcast.250, bf16[512,2048]{1,0:T(8,128)(2,1)} %bitcast.232), kind=kOutput, calls=%fused_computation.8 | convolution fusion | flops 1075838976 | bytes 4718592 | tf_op jit(solution)/shard_map/dot_general | solution.py:23
  106.5 1.7 fusion.1
  108.2 0.9 fusion.12
  109.1 2.6 multiply_convert_fusion
  111.7 77.4 %swap_2.1 = (bf16[4,128,2048]{2,1,0:T(8,128)(2,1)}, bf16[4,64,2048]{2,1,0:T(8,128)(2,1)}, bf16[4,64,256]{2,1,0:T(8,128)(2,1)}, bf16[4,128,2048]{2,1,0:T(8,128)(2,1)}) custom-call(bf16[4,128,2048]{2,1,0:T(8,128)(2,1)} %bitcast.242, bf16[4,64,2048]{2,1,0:T(8,128)(2,1)} %bitcast.247, bf16[4,64,256]{2,1,0:T(8,128)(2,1)} %bitcast.252, bf16[4,128,2048]{2,1,0:T(8,128)(2,1)} %bitcast.243), custom_call_target="tpu_custom_call" | custom-call | tf_op jit(solution)/shard_map/swap_2/pallas_call | solution.py:122
  189.0 4.1 %convert_bitcast_fusion = f32[128,4,2048]{2,0,1:T(8,128)} fusion(bf16[4,128,2048]{2,1,0:T(8,128)(2,1)} %get-tuple-element.23), kind=kLoop, calls=%fused_computation.4 | loop fusion | flops 1048576 | bytes 6291456 | tf_op jit(solution)/shard_map/convert_element_type | solution.py:464
  193.1 5.3 %copy.38 = f32[128,4,2048]{0,2,1:T(8,128)} copy(f32[128,4,2048]{2,0,1:T(8,128)} %convert_bitcast_fusion) | data formatting | bytes 8388608 | tf_op jit(solution)/shard_map/convert_element_type | solution.py:464
  198.5 2.5 convert_bitcast_fusion.1
  201.0 5.4 %copy.37 = f32[128,16,512]{0,2,1:T(8,128)} copy(f32[128,16,512]{2,0,1:T(8,128)} %convert_bitcast_fusion.1) | data formatting | bytes 8388608 | tf_op jit(solution)/shard_map/convert_element_type | solution.py:464
  206.4 3.9 %fusion = bf16[128,8192]{0,1:T(8,128)(2,1)S(1)} fusion(f32[128,4,2048]{0,2,1:T(8,128)} %copy.38, f32[128,16,512]{0,2,1:T(8,128)} %copy.37), kind=kLoop, calls=%fused_computation.3 | loop fusion | flops 2097152 | bytes 10485760 | tf_op jit(solution)/shard_map/convert_element_type | solution.py:464
  210.3 2.9 %copy.53 = bf16[128,8192]{1,0:T(8,128)(2,1)} copy(bf16[128,8192]{0,1:T(8,128)(2,1)S(1)} %fusion) | data formatting | bytes 4194304
  213.2 2.3 convert_reduce_fusion
  216.3 1.5 copy.54
  217.8 1.8 bitcast_subtract_fusion.1
  219.7 1.4 copy-done.4
  221.6 1.3 pad_maximum_fusion.2
  224.7 2.1 fusion.28
  226.9 1.1 broadcast_select_fusion.refs_0_
  229.2 0.9 broadcast_select_fusion.1.refs_1_
  230.9 39.4 %swap_3.1 = (bf16[4,2,32,2048]{3,2,1,0:T(8,128)(2,1)}, bf16[4,32,2048]{2,1,0:T(8,128)(2,1)}, bf16[4,32,256]{2,1,0:T(8,128)(2,1)}) custom-call(bf16[4,2,32,2048]{3,2,1,0:T(8,128)(2,1)} %broadcast_select_fusion.refs_0_, bf16[4,32,2048]{2,1,0:T(8,128)(2,1)} %broadcast_select_fusion.1.refs_1_, bf16[4,32,256]{2,1,0:T(8,128)(2,1)} %broadcast_select_fusion.5.refs_2_), custom_call_target="tpu_custom_call" | custom-call | tf_op jit(solution)/shard_map/swap_3/pallas_call | solution.py:122
  278.8 1.3 constant_dynamic-slice_fusion.11
  280.1 1.1 pad_maximum_fusion.3
  281.3 0.9 pad_maximum_fusion.5
  (83 shorter events, 11.0 us)
Async XLA Ops:
  0.6 0.7 copy-start
  3.9 1.6 copy-start.13
  5.5 2.5 copy-start.14
  85.4 2.6 copy-start.1
  88.0 1.4 copy-start.8
  89.4 1.9 copy-start.10
  102.0 4.4 %copy-start.16 = (bf16[128,512]{1,0:T(8,128)(2,1)S(1)}, bf16[128,512]{1,0:T(8,128)(2,1)}, u32[]{:S(2)}) copy-start(bf16[128,512]{1,0:T(8,128)(2,1)} %low_sums.1) | copy-start | bytes 393220
  102.0 4.4 %copy-start.11 = (bf16[512,2048]{1,0:T(8,128)(2,1)S(1)}, bf16[512,2048]{1,0:T(8,128)(2,1)}, u32[]{:S(2)}) copy-start(bf16[512,2048]{1,0:T(8,128)(2,1)} %param.13) | copy-start | bytes 6291460
  106.5 2.6 copy-start.9
  213.2 2.5 copy-start.2
  215.4 2.3 copy-start.3
  216.2 1.5 copy-start.19
  217.7 1.8 copy-start.12
  219.6 1.6 copy-start.4
  219.7 3.2 %copy-start.6 = (f32[64,2048]{1,0:T(8,128)}, f32[64,2048]{1,0:T(8,128)S(1)}, u32[]{:S(2)}) copy-start(f32[64,2048]{1,0:T(8,128)S(1)} %convert_reduce_fusion.1) | copy-start | bytes 1572868
  221.6 1.3 copy-start.17
  221.6 2.1 copy-start.20
  226.8 1.8 copy-start.5
  226.8 1.9 copy-start.7
  278.8 2.5 copy-start.15
  280.1 2.0 copy-start.18
where the time goes:
time: 284 us; the launch traced here: 283 us
  Pallas kernels  203 us (71%)
  local copies, waits for them, and re-layouts  30.4 us (11%)
  other arithmetic  29.2 us (10%)
  matrix products  11.8 us (4%)
  between operations  8.79 us (3%)
    pallas_call x2, Pallas kernels, swap(): pl.pallas_call(functools.partial(swap_kernel, sizes, axes), out_shape=[ja...  117 us
    pallas_call x1, Pallas kernels, main_call(): pl.pallas_call(functools.partial(main_kernel, groups, n), out_shape=[s((s...  77.3 us
    dot_general x7, matrix products, dot(): lax.dot_general(a, b, (((ca,), (cb,)), ((), ())), preferred_element_type=...  11.8 us
    convert_element_type x2, local copies, waits for them, and re-layouts, body(): input_cotangent = (base.astype(F32) + lora_cols.astype(F32)).astype(BF16)  10.7 us
    convert_element_type x3, other arithmetic, body(): input_cotangent = (base.astype(F32) + lora_cols.astype(F32)).astype(BF16)  10.5 us
    pallas_call x1, Pallas kernels, add_everywhere(): pl.pallas_call(functools.partial(low_kernel, n), out_shape=jax.ShapeDtype...  8.4 us
    unnamed x44, local copies, waits for them, and re-layouts  7.03 us

commit v1 on v0

--- a/solution.py
+++ b/solution.py
@@ -21,19 +21,6 @@
 
 def dot(a, b, ca, cb):
     return lax.dot_general(a, b, (((ca,), (cb,)), ((), ())), preferred_element_type=F32)
-
-
-def adam_parts(packed_state, gradient, counts):
-    master = packed_state[:, 0]
-    first = BETA_ONE * packed_state[:, 1] + (1.0 - BETA_ONE) * gradient
-    second = BETA_TWO * packed_state[:, 2] + (1.0 - BETA_TWO) * gradient * gradient
-    shaped = counts.astype(F32).reshape((-1,) + (1,) * (gradient.ndim - 1))
-    fix_one = 1.0 - jnp.exp(shaped * math.log(BETA_ONE))
-    fix_two = 1.0 - jnp.exp(shaped * math.log(BETA_TWO))
-    master = master - LEARN_RATE * (
-        first / fix_one / (jnp.sqrt(second / fix_two) + ADAM_EPSILON) + WEIGHT_DECAY * master
-    )
-    return master, first, second
 
 
 MESH = pl.DeviceIdType.MESH
@@ -128,6 +115,158 @@
         compiler_params=pltpu.CompilerParams(collective_id=ident, has_side_effects=True),
         name="swap_%d" % ident,
     )(*arrays)
+
+
+def line_kernel(sizes, chunks, k, *refs):
+    parts, lora, sums, lora_came = refs[:k], refs[k], refs[k + 1 : 2 * k + 1], refs[2 * k + 1]
+    scratch = refs[2 * k + 2 :]
+    lora_send, lora_recv = scratch[:2]
+    m = len(chunks)
+    out_bufs, in_bufs = scratch[2 : 2 + m], scratch[2 + m : 2 + 2 * m]
+    sends, recvs = scratch[2 + 2 * m : 2 + 3 * m], scratch[2 + 3 * m : 2 + 4 * m]
+    n = sizes["dp"]
+    g = lax.axis_index("dp")
+    meet(sizes)
+    jobs = [
+        (
+            "tensor",
+            sizes["tensor"],
+            lambda p: lora.at[p],
+            lambda p: lora_came.at[:, pl.ds(pl.multiple_of(p * lora.shape[2], lora.shape[2]), lora.shape[2])],
+            lora_send,
+            lora_recv,
+        )
+    ]
+    launch(jobs)
+
+    def hop(c, way, s):
+        ahead = lax.rem(g + 1, n) if way == 0 else lax.rem(g + n - 1, n)
+        return pltpu.make_async_remote_copy(
+            src_ref=out_bufs[c].at[way, s],
+            dst_ref=in_bufs[c].at[way, s],
+            send_sem=sends[c].at[way, s],
+            recv_sem=recvs[c].at[way, s],
+            device_id={"dp": ahead},
+            device_id_type=MESH,
+        )
+
+    place = (g, n - 1 - g)
+    for s in range(1, n):
+        for way in (0, 1):
+
+            @pl.when(place[way] < s)
+            def _():
+                goal = g + (n - s) if way == 0 else g - (n - s)
+                for c, (i, lo, rows) in enumerate(chunks):
+                    term = parts[i][goal, lo : lo + rows]
+
+                    @pl.when(place[way] == 0)
+                    def _():
+                        out_bufs[c][way, s] = term
+
+                    if s > 1:
+
+                        @pl.when(place[way] > 0)
+                        def _():
+                            hop(c, way, s - 1).wait_recv()
+                            out_bufs[c][way, s] = (
+                                term.astype(F32) + in_bufs[c][way, s - 1].astype(F32)
+                            ).astype(BF16)
+
+                    hop(c, way, s).start()
+
+    for c, (i, lo, rows) in enumerate(chunks):
+        sums[i][lo : lo + rows] = parts[i][g, lo : lo + rows].astype(F32)
+        for way in (0, 1):
+
+            @pl.when(place[way] > 0)
+            def _():
+                hop(c, way, n - 1).wait_recv()
+                sums[i][lo : lo + rows] = sums[i][lo : lo + rows] + in_bufs[c][way, n - 1].astype(F32)
+
+    for s in range(1, n):
+        for way in (0, 1):
+
+            @pl.when(place[way] < s)
+            def _():
+                for c in range(m):
+                    hop(c, way, s).wait_send()
+
+    finish(jobs)
+
+
+def line_sums(parts, lora, sizes, rows):
+    k = len(parts)
+    chunks = [(i, lo, rows) for i, a in enumerate(parts) for lo in range(0, a.shape[1], rows)]
+    bufs = [pltpu.VMEM((2, sizes["dp"], r, parts[i].shape[2]), BF16) for i, _, r in chunks]
+    sems = [DMA((2, sizes["dp"])) for _ in chunks]
+    n = sizes["tensor"]
+    return pl.pallas_call(
+        functools.partial(line_kernel, sizes, chunks, k),
+        out_shape=[jax.ShapeDtypeStruct(a.shape[1:], F32) for a in parts]
+        + [jax.ShapeDtypeStruct((lora.shape[1], lora.shape[0] * lora.shape[2]), BF16)],
+        in_specs=[VMEM] * k + [ANY],
+        out_specs=[VMEM] * k + [ANY],
+        scratch_shapes=[DMA((n,)), DMA((n,))] + bufs + bufs + sems + sems,
+        compiler_params=pltpu.CompilerParams(
+            collective_id=2, has_side_effects=True, vmem_limit_bytes=48 * 1024 * 1024
+        ),
+        name="line_sums",
+    )(*parts, lora)
+
+
+def adam_kernel(split, fix, row, state, grad, *outs):
+    owned = state.shape[0]
+    fresh = []
+    for s in range(owned):
+        gradient = grad[s]
+        master = state[s, 0]
+        first = BETA_ONE * state[s, 1] + (1.0 - BETA_ONE) * gradient
+        second = BETA_TWO * state[s, 2] + (1.0 - BETA_TWO) * gradient * gradient
+        master = master - LEARN_RATE * (
+            first / fix[0, s] / (jnp.sqrt(second / fix[1, s]) + ADAM_EPSILON)
+            + WEIGHT_DECAY * master
+        )
+        if split:
+            outs[0][s] = master
+            outs[1][s, 0] = first
+            outs[1][s, 1] = second
+        else:
+            outs[0][s, 0] = master
+            outs[0][s, 1] = first
+            outs[0][s, 2] = second
+        fresh.append(master.astype(BF16))
+    for r in range(outs[-1].shape[0]):
+        outs[-1][r] = fresh[0]
+        for s in range(1, owned):
+
+            @pl.when(row[r] == s)
+            def _():
+                outs[-1][r] = fresh[s]
+
+
+def adam(state, grad, fix, row, split):
+    owned, _, rows, width = state.shape
+    cols = min(512, width)
+    kinds = [((owned, rows, width), F32), ((owned, 2, rows, width), F32)]
+    if not split:
+        kinds = [((owned, 3, rows, width), F32)]
+    kinds.append(((row.shape[0], rows, width), BF16))
+
+    def spec(shape):
+        lead = len(shape) - 1
+        return pl.BlockSpec(tuple(shape[:-1]) + (cols,), lambda j: (0,) * lead + (j,))
+
+    smem = pl.BlockSpec(memory_space=pltpu.SMEM)
+    return pl.pallas_call(
+        functools.partial(adam_kernel, split),
+        grid=(width // cols,),
+        out_shape=[jax.ShapeDtypeStruct(a, d) for a, d in kinds],
+        in_specs=[smem, smem, spec(state.shape), spec(grad.shape)],
+        out_specs=[spec(a) for a, _ in kinds],
+        compiler_params=pltpu.CompilerParams(vmem_limit_bytes=48 * 1024 * 1024),
+        name="adam",
+    )(fix, row, state, grad)
 
 
 def low_kernel(n, part, out, came, send, recv):
@@ -282,7 +421,7 @@
         for k in range(1, chips):
             far_copy(k, j).wait()
             total = total + far[k, j].astype(F32)
-        out[j] = total.astype(BF16)
+        out[:, pl.ds(pl.multiple_of(j * cols, cols), cols)] = total.astype(BF16)
         return carry
 
     lax.fori_loop(0, steps, last, 0)
@@ -300,7 +439,7 @@
     return pl.pallas_call(
         functools.partial(main_kernel, groups, n),
         out_shape=[
-            s((steps, rows, cols), BF16),
+            s((rows, steps * cols), BF16),
             s((n, rows, width), BF16),
             s((groups,) + own_wide.shape, BF16),
             s((groups,) + own_value.shape, BF16),
@@ -419,38 +558,38 @@
     value_part = (ADAPTER_SCALE * dot(spread(low_h[rank:]), value_cotangent, 1, 0)).astype(BF16)
     lora = (ADAPTER_SCALE * dot(low_u_at, work_down, 0, 0)).astype(BF16)
 
-    down_came, query_came, value_came, lora_came = swap(
+    down_grad, query_grad, value_grad, lora_came = line_sums(
         [
             down_part.reshape(G, owned * 2 * rank, width),
             query_part.reshape(G, owned * rank, width),
             value_part.reshape(G, owned * rank, value_here),
-            lora.reshape(T, rows, width),
         ],
-        ("dp", "dp", "dp", "tensor"),
+        lora.reshape(T, rows, width),
         sizes,
-        2,
-    )
-    down_grad = jnp.sum(down_came.astype(F32), axis=0).reshape(owned, 2, rank, width)
-    query_grad = jnp.sum(query_came.astype(F32), axis=0).reshape(owned, rank, width)
-    value_grad = jnp.sum(value_came.astype(F32), axis=0).reshape(owned, rank, value_here)
-
-    d_master, d_first, d_second = adam_parts(down_state, down_grad, slot_step)
-    q_master, q_first, q_second = adam_parts(query_state, query_grad, slot_step)
-    v_master, v_first, v_second = adam_parts(value_state, value_grad, slot_step)
+        owned * rank,
+    )
 
     serve_rows = owner_slot[serve_tenant].reshape(G, served_here)
     row = jnp.sum(jnp.where(serve_rows // owned == g, serve_rows % owned, 0), axis=1)
-
-    def wanted(master):
-        fresh = master.astype(BF16)[None]
-        pick_row = row.reshape((-1,) + (1,) * (fresh.ndim - 2))
-        out = fresh[:, 0]
-        for r in range(1, owned):
-            out = jnp.where(pick_row == r, fresh[:, r], out)
-        return out
-
+    counts = slot_step.astype(F32)
+    fix = jnp.stack(
+        [1.0 - jnp.exp(counts * math.log(BETA_ONE)), 1.0 - jnp.exp(counts * math.log(BETA_TWO))]
+    )
+    d_master, d_moments, d_wanted = adam(
+        down_state.reshape(owned, 3, 2 * rank, width),
+        down_grad.reshape(owned, 2 * rank, width),
+        fix,
+        row,
+        True,
+    )
+    new_query, q_wanted = adam(
+        query_state, query_grad.reshape(owned, rank, width), fix, row, False
+    )
+    new_value, v_wanted = adam(
+        value_state, value_grad.reshape(owned, rank, value_here), fix, row, False
+    )
     down_new, query_new, value_new = swap(
-        [wanted(d_master), wanted(q_master), wanted(v_master)], ("dp",) * 3, sizes, 3
+        [d_wanted, q_wanted, v_wanted], ("dp",) * 3, sizes, 3
     )
     owner = lax.dynamic_index_in_dim(serve_rows, g, 0, False) // owned
 
@@ -459,17 +598,15 @@
             [lax.dynamic_index_in_dim(came, owner[q], 0, False) for q in range(served_here)]
         )
 
-    lora_cols = jnp.swapaxes(lora_came, 0, 1).reshape(rows, T * width)
-    base = jnp.swapaxes(frozen, 0, 1).reshape(rows, T * width)
-    input_cotangent = (base.astype(F32) + lora_cols.astype(F32)).astype(BF16)
+    input_cotangent = (frozen.astype(F32) + lora_came.astype(F32)).astype(BF16)
 
     return (
         input_cotangent,
-        jnp.stack([d_first, d_second], axis=1),
-        d_master,
-        jnp.stack([q_master, q_first, q_second], axis=1),
-        jnp.stack([v_master, v_first, v_second], axis=1),
-        served(down_new),
+        d_moments.reshape(owned, 2, 2, rank, width),
+        d_master.reshape(owned, 2, rank, width),
+        new_query,
+        new_value,
+        served(down_new).reshape(served_here, 2, rank, width),
         served(query_new),
         served(value_new),
     )

time: 284 us -> 240 us (0.85)
  other arithmetic: 29.2 us -> 7.68 us
  local copies, waits for them, and re-layouts: 30.4 us -> 16.8 us
  Pallas kernels: 203 us -> 196 us
    pallas_call x2 -> x1, Pallas kernels: 117 us -> 38.3 us  [swap(): pl.pallas_call(functools.partial(swap_kernel, sizes, axes), out_shape=[ja...]
    pallas_call x1 -> x5, Pallas kernels: 77.3 us -> 149 us  [the longest x1 77.3 us: main_call(): pl.pallas_call(functools.partial(main_kernel, groups, n), out_shape=[s((r...]
    convert_element_type x6 -> x1, other arithmetic: 13.2 us -> 1.82 us  [body(): input_cotangent = (frozen.astype(F32) + lora_came.astype(F32)).astype(BF16)]
    convert_element_type x2 -> x0, local copies, waits for them, and re-layouts: 10.7 us -> none  [body(): input_cotangent = (base.astype(F32) + lora_cols.astype(F32)).astype(BF16)]
    unnamed x44 -> x50, local copies, waits for them, and re-layouts: 7.03 us -> 4.69 us
where the time goes in v1:
time: 240 us; the launch traced here: 239 us
  Pallas kernels  196 us (82%)
  local copies, waits for them, and re-layouts  16.8 us (7%)
  matrix products  10.2 us (4%)
  between operations  8.68 us (4%)
  other arithmetic  7.68 us (3%)
    pallas_call x1, Pallas kernels, main_call(): pl.pallas_call(functools.partial(main_kernel, groups, n), out_shape=[s((r...  77.3 us
    pallas_call x1, Pallas kernels, line_sums(): pl.pallas_call(functools.partial(line_kernel, sizes, chunks, k), out_shap...  64.4 us
    pallas_call x1, Pallas kernels, swap(): pl.pallas_call(functools.partial(swap_kernel, sizes, axes), out_shape=[ja...  38.3 us
    dot_general x7, matrix products, dot(): lax.dot_general(a, b, (((ca,), (cb,)), ((), ())), preferred_element_type=...  10.2 us
    pallas_call x1, Pallas kernels, add_everywhere(): pl.pallas_call(functools.partial(low_kernel, n), out_shape=jax.ShapeDtype...  8.4 us
    pallas_call x3, Pallas kernels, adam(): pl.pallas_call(functools.partial(adam_kernel, split), grid=(width // cols...  7.18 us

profile of v1, /device:TPU:0, one launch (start us, length us, event | category | flops | bytes accessed | tf_op | source)
XLA Modules:
  0.0 239.0 jit_solution(6570098889374466987)
XLA Ops:
  0.6 0.7 compare_select_fusion.1
  1.3 0.6 gather_fusion
  2.1 1.8 constant_dynamic-slice_fusion.20
  3.9 1.6 pad_maximum_fusion.lhs_q
  5.6 1.1 copy-done.1
  6.7 1.1 slice.73
  7.9 77.3 %frozen_and_gathers.1 = (bf16[128,8192]{1,0:T(8,128)(2,1)S(1)}, bf16[4,128,2048]{2,1,0:T(8,128)(2,1)S(1)}, bf16[4,192,2048]{2,1,0:T(8,128)(2,1)}, bf16[4,64,256]{2,1,0:T(8,128)(2,1)S(1)}) custom-call(bf16[512,2048]{1,0:T(8,128)(2,1)} %pad_maximum_fusion.lhs_q, bf16[512,256]{1,0:T(8,128)(2,1)S(1)} %pad_maximum_fusion.4.lhs_v, ...), custom_call_target="tpu_custom_call" | custom-call | tf_op jit(solution)/shard_map/frozen_and_gathers/pallas_call | solution.py:439
  85.3 3.3 %slice.54 = bf16[4,128,2048]{2,1,0:T(8,128)(2,1)S(1)} slice(bf16[4,192,2048]{2,1,0:T(8,128)(2,1)} %get-tuple-element.27), slice={[0:4], [64:192], [0:2048]} | slice | bytes 4194304 | tf_op jit(solution)/shard_map/slice | solution.py:531
  88.7 1.3 fusion.3
  90.3 1.5 slice.53
  91.9 0.7 fusion.8
  92.6 0.7 pad_maximum_fusion.5.part
  93.3 8.4 %low_sums.1 = bf16[128,512]{1,0:T(8,128)(2,1)} custom-call(bf16[128,512]{1,0:T(8,128)(2,1)} %pad_maximum_fusion.5.part), custom_call_target="tpu_custom_call" | custom-call | tf_op jit(solution)/shard_map/low_sums/pallas_call | solution.py:290
  101.7 0.8 slice.55
  102.6 4.4 %multiply_convert_fusion.1 = bf16[512,2048]{1,0:T(8,128)(2,1)} fusion(bf16[512,512]{1,0:T(8,128)(2,1)S(1)} %bitcast.77, bf16[512,2048]{1,0:T(8,128)(2,1)} %bitcast.66), kind=kOutput, calls=%fused_computation.4 | convolution fusion | flops 1075838976 | bytes 4718592 | tf_op jit(solution)/shard_map/dot_general | solution.py:23
  107.1 0.7 fusion
  108.7 2.6 %multiply_convert_fusion = bf16[512,2048]{1,0:T(8,128)(2,1)} fusion(bf16[512,512]{1,0:T(8,128)(2,1)S(1)} %bitcast.78, bf16[512,2048]{1,0:T(8,128)(2,1)S(1)} %bitcast.70), kind=kOutput, calls=%fused_computation.3 | convolution fusion | flops 1075838976 | bytes 4718592 | tf_op jit(solution)/shard_map/dot_general | solution.py:23
  111.3 64.4 %line_sums.1 = (f32[128,2048]{1,0:T(8,128)S(1)}, f32[64,2048]{1,0:T(8,128)S(1)}, f32[64,256]{1,0:T(8,128)S(1)}, bf16[128,8192]{1,0:T(8,128)(2,1)S(1)}) custom-call(bf16[4,128,2048]{2,1,0:T(8,128)(2,1)} %bitcast.71, bf16[4,64,2048]{2,1,0:T(8,128)(2,1)S(1)} %bitcast.60, bf16[4,64,256]{2,1,0:T(8,128)(2,1)S(1)} %bitcast.62, bf16[4,128,2048]{2,1,0:T(8,128)(2,1)} %bitcast.72), custom_call_target="tpu_custom_call" | custom-call | tf_op jit(solution)/shard_map/line_sums/pallas_call | solution.py:204
  175.8 1.8 add_convert_fusion
  177.7 0.7 gather_fusion.1
  178.6 1.2 copy-done.6
  179.8 3.3 %adam.3 = (f32[2,64,2048]{2,1,0:T(8,128)}, f32[2,2,64,2048]{3,2,1,0:T(8,128)}, bf16[4,64,2048]{2,1,0:T(8,128)(2,1)S(1)}) custom-call(f32[2,2]{1,0:T(2,128)S(1)} %pad_maximum_fusion.7.fix, s32[4]{0:T(128)S(1)} %fusion.15.row, f32[2,3,64,2048]{3,2,1,0:T(8,128)S(1)} %bitcast.58, f32[2,64,2048]{2,1,0:T(8,128)S(1)} %bitcast.59), custom_call_target="tpu_custom_call" | custom-call | tf_op jit(solution)/shard_map/adam/pallas_call | solution.py:261
  183.1 2.6 %adam.4 = (f32[2,3,32,2048]{3,2,1,0:T(8,128)}, bf16[4,32,2048]{2,1,0:T(8,128)(2,1)S(1)}) custom-call(f32[2,2]{1,0:T(2,128)S(1)} %pad_maximum_fusion.7.fix, s32[4]{0:T(128)S(1)} %fusion.15.row, f32[2,3,32,2048]{3,2,1,0:T(8,128)S(1)} %copy-done.2, f32[2,32,2048]{2,1,0:T(8,128)S(1)} %bitcast.61), custom_call_target="tpu_custom_call" | custom-call | tf_op jit(solution)/shard_map/adam/pallas_call | solution.py:261
  185.7 0.8 copy-done.8
  186.5 1.3 adam.5
  187.8 0.6 copy-done.12
  188.4 38.3 %swap_3.1 = (bf16[4,64,2048]{2,1,0:T(8,128)(2,1)}, bf16[4,32,2048]{2,1,0:T(8,128)(2,1)}, bf16[4,32,256]{2,1,0:T(8,128)(2,1)}) custom-call(bf16[4,64,2048]{2,1,0:T(8,128)(2,1)} %copy-done.7, bf16[4,32,2048]{2,1,0:T(8,128)(2,1)} %copy-done.8, bf16[4,32,256]{2,1,0:T(8,128)(2,1)} %copy-done.12), custom_call_target="tpu_custom_call" | custom-call | tf_op jit(solution)/shard_map/swap_3/pallas_call | solution.py:109
  226.7 0.6 fusion.19
  235.0 1.3 constant_dynamic-slice_fusion.11
  236.3 1.1 pad_maximum_fusion.1
  237.5 0.9 pad_maximum_fusion.3
  238.3 0.6 pad_maximum_fusion.6
  (69 shorter events, 2.2 us)
Async XLA Ops:
  0.6 0.7 copy-start
  3.9 1.6 copy-start.18
  3.9 2.7 %copy-start.1 = (f32[2,3,2,32,2048]{4,3,2,1,0:T(8,128)S(1)}, f32[2,3,2,32,2048]{4,3,2,1,0:T(8,128)}, u32[]{:S(2)}) copy-start(f32[2,3,2,32,2048]{4,3,2,1,0:T(8,128)} %param.20) | copy-start | bytes 9437188
  5.5 2.4 copy-start.11
  85.3 3.4 %copy-start.3 = (bf16[128,8192]{1,0:T(8,128)(2,1)}, bf16[128,8192]{1,0:T(8,128)(2,1)S(1)}, u32[]{:S(2)}) copy-start(bf16[128,8192]{1,0:T(8,128)(2,1)S(1)} %get-tuple-element.26) | copy-start | bytes 6291460
  85.3 3.4 %copy-start.13 = (bf16[4,128,2048]{2,1,0:T(8,128)(2,1)}, bf16[4,128,2048]{2,1,0:T(8,128)(2,1)S(1)}, u32[]{:S(2)}) copy-start(bf16[4,128,2048]{2,1,0:T(8,128)(2,1)S(1)} %get-tuple-element.29) | copy-start | bytes 6291460
  88.6 1.3 copy-start.14
  90.0 1.9 copy-start.16
  102.6 4.4 %copy-start.21 = (bf16[128,512]{1,0:T(8,128)(2,1)S(1)}, bf16[128,512]{1,0:T(8,128)(2,1)}, u32[]{:S(2)}) copy-start(bf16[128,512]{1,0:T(8,128)(2,1)} %low_sums.1) | copy-start | bytes 393220
  102.6 4.4 %copy-start.17 = (bf16[512,2048]{1,0:T(8,128)(2,1)S(1)}, bf16[512,2048]{1,0:T(8,128)(2,1)}, u32[]{:S(2)}) copy-start(bf16[512,2048]{1,0:T(8,128)(2,1)} %param.13) | copy-start | bytes 6291460
  107.0 0.9 copy-start.19
  107.0 1.6 copy-start.15
  111.3 64.5 %copy-start.4 = (bf16[128,8192]{1,0:T(8,128)(2,1)S(1)}, bf16[128,8192]{1,0:T(8,128)(2,1)}, u32[]{:S(2)}) copy-start(bf16[128,8192]{1,0:T(8,128)(2,1)} %copy-done.3) | copy-start | bytes 6291460
  175.7 1.9 copy-start.5
  175.7 1.9 copy-start.9
  175.8 1.8 copy-start.23
  175.8 1.9 copy-start.24
  178.5 1.2 copy-start.6
  179.8 3.3 %copy-start.2 = (f32[2,3,32,2048]{3,2,1,0:T(8,128)S(1)}, f32[2,3,32,2048]{3,2,1,0:T(8,128)}, u32[]{:S(2)}) copy-start(f32[2,3,32,2048]{3,2,1,0:T(8,128)} %state.2) | copy-start | bytes 4718596
  179.8 3.3 %copy-start.10 = (f32[64,2048]{1,0:T(8,128)S(1)}, f32[64,2048]{1,0:T(8,128)}, u32[]{:S(2)}) copy-start(f32[64,2048]{1,0:T(8,128)} %copy-done.9) | copy-start | bytes 1572868
  183.1 2.6 %copy-start.7 = (bf16[4,64,2048]{2,1,0:T(8,128)(2,1)}, bf16[4,64,2048]{2,1,0:T(8,128)(2,1)S(1)}, u32[]{:S(2)}) copy-start(bf16[4,64,2048]{2,1,0:T(8,128)(2,1)S(1)} %get-tuple-element.38.refs_0_) | copy-start | bytes 3145732
  185.7 0.8 copy-start.8
  187.8 0.6 copy-start.12
  235.0 2.5 %copy-start.20 = (bf16[4,32,2048]{2,1,0:T(8,128)(2,1)S(1)}, bf16[4,32,2048]{2,1,0:T(8,128)(2,1)}, u32[]{:S(2)}) copy-start(bf16[4,32,2048]{2,1,0:T(8,128)(2,1)} %get-tuple-element.42) | copy-start | bytes 1572868
  236.3 2.0 copy-start.22

commit v2 on v1

--- a/solution.py
+++ b/solution.py
@@ -269,6 +269,31 @@
     )(fix, row, state, grad)
 
 
+def slots_kernel(owner, *refs):
+    k = len(refs) // 2
+    for came, out in zip(refs[:k], refs[k:]):
+        for q in range(out.shape[0]):
+            for p in range(came.shape[0]):
+
+                @pl.when(owner[q] == p)
+                def _():
+                    out[q] = came[p]
+
+
+def served(owner, arrays):
+    k = len(arrays)
+    return pl.pallas_call(
+        slots_kernel,
+        out_shape=[
+            jax.ShapeDtypeStruct(owner.shape + a.shape[1:], a.dtype) for a in arrays
+        ],
+        in_specs=[pl.BlockSpec(memory_space=pltpu.SMEM)] + [VMEM] * k,
+        out_specs=[VMEM] * k,
+        compiler_params=pltpu.CompilerParams(vmem_limit_bytes=48 * 1024 * 1024),
+        name="serving_slots",
+    )(owner, *arrays)
+
+
 def low_kernel(n, part, out, came, send, recv):
     meet({"tensor": n})
     for s in range(1, n):
@@ -306,11 +331,13 @@
     query_matrix,
     value_matrix,
     activations,
-    own_wide,
+    own_query,
+    own_down,
     own_value,
     out,
     feats,
-    all_wide,
+    all_query,
+    all_down,
     all_value,
     weight,
     weight_v,
@@ -326,8 +353,10 @@
     far_recv,
     feat_send,
     feat_recv,
-    wide_send,
-    wide_recv,
+    query_send,
+    query_recv,
+    down_send,
+    down_recv,
     value_send,
     value_recv,
 ):
@@ -360,7 +389,8 @@
             feat_recv,
         ),
         ("dp", groups, lambda p: own_value, lambda p: all_value.at[p], value_send, value_recv),
-        ("dp", groups, lambda p: own_wide, lambda p: all_wide.at[p], wide_send, wide_recv),
+        ("dp", groups, lambda p: own_query, lambda p: all_query.at[p], query_send, query_recv),
+        ("dp", groups, lambda p: own_down, lambda p: all_down.at[p], down_send, down_recv),
     ]
     launch(jobs)
 
@@ -428,7 +458,7 @@
     finish(jobs)
 
 
-def main_call(groups, n, lhs_q, lhs_v, query_matrix, value_matrix, activations, own_wide, own_value):
+def main_call(groups, n, lhs_q, lhs_v, query_matrix, value_matrix, activations, own_query, own_down, own_value):
     tokens, width = lhs_q.shape
     rows = activations.shape[0]
     cols = 512
@@ -441,11 +471,12 @@
         out_shape=[
             s((rows, steps * cols), BF16),
             s((n, rows, width), BF16),
-            s((groups,) + own_wide.shape, BF16),
+            s((groups,) + own_query.shape, BF16),
+            s((groups,) + own_down.shape, BF16),
             s((groups,) + own_value.shape, BF16),
         ],
-        in_specs=[VMEM, VMEM] + [ANY] * 5,
-        out_specs=[VMEM, ANY, ANY, ANY],
+        in_specs=[VMEM, VMEM] + [ANY] * 6,
+        out_specs=[VMEM, ANY, ANY, ANY, ANY],
         scratch_shapes=[
             pltpu.VMEM((2, cols, width), BF16),
             pltpu.VMEM((2, cols, lhs_v.shape[1]), BF16),
@@ -465,12 +496,14 @@
             DMA((groups,)),
             DMA((groups,)),
             DMA((groups,)),
+            DMA((groups,)),
+            DMA((groups,)),
         ],
         compiler_params=pltpu.CompilerParams(
             collective_id=0, has_side_effects=True, vmem_limit_bytes=48 * 1024 * 1024
         ),
         name="frozen_and_gathers",
-    )(lhs_q, lhs_v, query_matrix, value_matrix, activations, own_wide, own_value)
+    )(lhs_q, lhs_v, query_matrix, value_matrix, activations, own_query, own_down, own_value)
 
 
 def body(
@@ -502,9 +535,8 @@
     block_len = tokens // block_tenant.shape[0]
     served_here = serve_tenant.shape[0] // G
 
-    own_wide = jnp.concatenate(
-        [query_state[:, 0].reshape(owned * rank, width), down_state[:, 0].reshape(-1, width)], axis=0
-    ).astype(BF16)
+    own_query = query_state[:, 0].astype(BF16).reshape(owned * rank, width)
+    own_down = down_state[:, 0].astype(BF16).reshape(owned * 2 * rank, width)
     own_value = value_state[:, 0].astype(BF16).reshape(owned * rank, value_here)
 
     def ordered(a):
@@ -515,7 +547,7 @@
         ]
         return jnp.concatenate(cut, axis=0)
 
-    frozen, feats, all_wide, all_value = main_call(
+    frozen, feats, all_query, all_down, all_value = main_call(
         G,
         T,
         ordered(query_cotangent),
@@ -523,12 +555,13 @@
         query_matrix,
         value_matrix,
         activations,
-        own_wide,
+        own_query,
+        own_down,
         own_value,
     )
     feats = feats.reshape(tokens, width)
-    work_query = all_wide[:, : owned * rank].reshape(slots * rank, width)
-    work_down = all_wide[:, owned * rank :].reshape(slots * 2 * rank, width)
+    work_query = all_query.reshape(slots * rank, width)
+    work_down = all_down.reshape(slots * 2 * rank, width)
     work_value = all_value.reshape(slots * rank, value_here)
 
     position = jnp.repeat(owner_slot[block_tenant], block_len)
@@ -593,10 +626,7 @@
     )
     owner = lax.dynamic_index_in_dim(serve_rows, g, 0, False) // owned
 
-    def served(came):
-        return jnp.stack(
-            [lax.dynamic_index_in_dim(came, owner[q], 0, False) for q in range(served_here)]
-        )
+    served_down, served_query, served_value = served(owner, [down_new, query_new, value_new])
 
     input_cotangent = (frozen.astype(F32) + lora_came.astype(F32)).astype(BF16)
 
@@ -606,9 +636,9 @@
         d_master.reshape(owned, 2, rank, width),
         new_query,
         new_value,
-        served(down_new).reshape(served_here, 2, rank, width),
-        served(query_new),
-        served(value_new),
+        served_down.reshape(served_here, 2, rank, width),
+        served_query,
+        served_value,
     )
 
 

time: 240 us -> 230 us (0.958)
  between operations: 8.68 us -> 0.98 us
  local copies, waits for them, and re-layouts: 16.8 us -> 12 us
  matrix products: 10.2 us -> 13.2 us
  other arithmetic: 7.68 us -> 5 us
    slice x5 -> x2, local copies, waits for them, and re-layouts: 6.56 us -> 1.32 us  [the longest x1 1.26 us: body(): own_query = query_state[:, 0].astype(BF16).reshape(owned * rank, width)]
    dot_general x7, matrix products: 10.2 us -> 13.2 us  [dot(): lax.dot_general(a, b, (((ca,), (cb,)), ((), ())), preferred_element_type=...]
    another operation x3 -> x0, other arithmetic: 2.61 us -> none  [served(): jnp.stack([lax.dynamic_index_in_dim(came, owner[q], 0, False) for q in ra...]
    unnamed x50 -> x48, local copies, waits for them, and re-layouts: 4.69 us -> 6.49 us
where the time goes in v2:
time: 230 us; the launch traced here: 229 us
  Pallas kernels  198 us (86%)
  matrix products  13.2 us (6%)
  local copies, waits for them, and re-layouts  12 us (5%)
  other arithmetic  5 us (2%)
    pallas_call x1, Pallas kernels, main_call(): pl.pallas_call(functools.partial(main_kernel, groups, n), out_shape=[s((r...  77.4 us
    pallas_call x1, Pallas kernels, line_sums(): pl.pallas_call(functools.partial(line_kernel, sizes, chunks, k), out_shap...  64.5 us
    pallas_call x1, Pallas kernels, swap(): pl.pallas_call(functools.partial(swap_kernel, sizes, axes), out_shape=[ja...  38.3 us
    dot_general x7, matrix products, dot(): lax.dot_general(a, b, (((ca,), (cb,)), ((), ())), preferred_element_type=...  13.2 us
    pallas_call x1, Pallas kernels, add_everywhere(): pl.pallas_call(functools.partial(low_kernel, n), out_shape=jax.ShapeDtype...  8.4 us
    pallas_call x3, Pallas kernels, adam(): pl.pallas_call(functools.partial(adam_kernel, split), grid=(width // cols...  7.17 us
    unnamed x48, local copies, waits for them, and re-layouts  6.49 us

profile of v2, /device:TPU:0, one launch (start us, length us, event | category | flops | bytes accessed | tf_op | source)
XLA Modules:
  0.0 229.1 jit_solution(15772335846409471310)
XLA Ops:
  0.6 0.7 compare_select_fusion.1
  1.3 0.6 gather_fusion
  2.1 1.8 constant_dynamic-slice_fusion.8
  3.9 1.6 pad_maximum_fusion.lhs_q
  5.6 1.3 slice.41
  6.9 77.4 %frozen_and_gathers.1 = (bf16[128,8192]{1,0:T(8,128)(2,1)S(1)}, bf16[4,128,2048]{2,1,0:T(8,128)(2,1)}, bf16[4,64,2048]{2,1,0:T(8,128)(2,1)S(1)}, bf16[4,128,2048]{2,1,0:T(8,128)(2,1)}, bf16[4,64,256]{2,1,0:T(8,128)(2,1)S(1)}) custom-call(bf16[512,2048]{1,0:T(8,128)(2,1)} %pad_maximum_fusion.lhs_q, bf16[512,256]{1,0:T(8,128)(2,1)S(1)} %pad_maximum_fusion.1.lhs_v, ...), custom_call_target="tpu_custom_call" | custom-call | tf_op jit(solution)/shard_map/frozen_and_gathers/pallas_call | solution.py:469
  84.4 4.3 %fusion.3 = bf16[64,512]{1,0:T(8,128)(2,1)S(1)} fusion(bf16[8,64,2048]{2,1,0:T(8,128)(2,1)} %bitcast.72, bf16[512,2048,1]{1,0,2:T(8,128)(2,1)} %bitcast.74, pred[8,512]{1,0:T(8,128)(4,1)S(1)} %iota_compare_fusion), kind=kOutput, calls=%fused_computation.11 | convolution fusion | flops 1074233344 | bytes 4263936 | tf_op jit(solution)/shard_map/dot_general | solution.py:23
  88.7 0.3 fusion.7
  89.0 0.8 fusion.8
  89.8 0.7 pad_maximum_fusion.2.part
  90.4 8.4 %low_sums.1 = bf16[128,512]{1,0:T(8,128)(2,1)} custom-call(bf16[128,512]{1,0:T(8,128)(2,1)} %pad_maximum_fusion.2.part), custom_call_target="tpu_custom_call" | custom-call | tf_op jit(solution)/shard_map/low_sums/pallas_call | solution.py:315
  98.8 0.8 slice.27
  99.7 4.4 %multiply_convert_fusion.1 = bf16[512,2048]{1,0:T(8,128)(2,1)} fusion(bf16[512,512]{1,0:T(8,128)(2,1)S(1)} %bitcast.68, bf16[512,2048]{1,0:T(8,128)(2,1)} %bitcast.75), kind=kOutput, calls=%fused_computation.4 | convolution fusion | flops 1075838976 | bytes 4718592 | tf_op jit(solution)/shard_map/dot_general | solution.py:23
  104.2 0.7 fusion
  104.9 0.1 copy-done.19
  105.0 0.2 fusion.11
  105.3 0.5 copy-done.21
  105.8 2.6 %multiply_convert_fusion = bf16[512,2048]{1,0:T(8,128)(2,1)} fusion(bf16[512,512]{1,0:T(8,128)(2,1)S(1)} %bitcast.69, bf16[512,2048]{1,0:T(8,128)(2,1)S(1)} %bitcast.73), kind=kOutput, calls=%fused_computation.3 | convolution fusion | flops 1075838976 | bytes 4718592 | tf_op jit(solution)/shard_map/dot_general | solution.py:23
  108.4 64.5 %line_sums.1 = (f32[128,2048]{1,0:T(8,128)S(1)}, f32[64,2048]{1,0:T(8,128)S(1)}, f32[64,256]{1,0:T(8,128)S(1)}, bf16[128,8192]{1,0:T(8,128)(2,1)S(1)}) custom-call(bf16[4,128,2048]{2,1,0:T(8,128)(2,1)} %bitcast.65, bf16[4,64,2048]{2,1,0:T(8,128)(2,1)S(1)} %bitcast.58, bf16[4,64,256]{2,1,0:T(8,128)(2,1)S(1)} %bitcast.60, bf16[4,128,2048]{2,1,0:T(8,128)(2,1)} %bitcast.66), custom_call_target="tpu_custom_call" | custom-call | tf_op jit(solution)/shard_map/line_sums/pallas_call | solution.py:204
  172.9 1.8 add_convert_fusion
  174.8 0.7 gather_fusion.1
  175.7 1.2 copy-done.6
  176.9 3.3 %adam.3 = (f32[2,64,2048]{2,1,0:T(8,128)}, f32[2,2,64,2048]{3,2,1,0:T(8,128)}, bf16[4,64,2048]{2,1,0:T(8,128)(2,1)S(1)}) custom-call(f32[2,2]{1,0:T(2,128)S(1)} %pad_maximum_fusion.3.fix, s32[4]{0:T(128)S(1)} %fusion.15.row, f32[2,3,64,2048]{3,2,1,0:T(8,128)S(1)} %bitcast.54, f32[2,64,2048]{2,1,0:T(8,128)S(1)} %bitcast.57), custom_call_target="tpu_custom_call" | custom-call | tf_op jit(solution)/shard_map/adam/pallas_call | solution.py:261
  180.2 2.6 %adam.4 = (f32[2,3,32,2048]{3,2,1,0:T(8,128)}, bf16[4,32,2048]{2,1,0:T(8,128)(2,1)S(1)}) custom-call(f32[2,2]{1,0:T(2,128)S(1)} %pad_maximum_fusion.3.fix, s32[4]{0:T(128)S(1)} %fusion.15.row, f32[2,3,32,2048]{3,2,1,0:T(8,128)S(1)} %copy-done.2, f32[2,32,2048]{2,1,0:T(8,128)S(1)} %bitcast.59), custom_call_target="tpu_custom_call" | custom-call | tf_op jit(solution)/shard_map/adam/pallas_call | solution.py:261
  182.8 0.8 copy-done.9
  183.6 1.3 adam.5
  184.9 0.6 copy-done.14
  185.5 38.3 %swap_3.1 = (bf16[4,64,2048]{2,1,0:T(8,128)(2,1)}, bf16[4,32,2048]{2,1,0:T(8,128)(2,1)}, bf16[4,32,256]{2,1,0:T(8,128)(2,1)}) custom-call(bf16[4,64,2048]{2,1,0:T(8,128)(2,1)} %copy-done.8, bf16[4,32,2048]{2,1,0:T(8,128)(2,1)} %copy-done.9, bf16[4,32,256]{2,1,0:T(8,128)(2,1)} %copy-done.14), custom_call_target="tpu_custom_call" | custom-call | tf_op jit(solution)/shard_map/swap_3/pallas_call | solution.py:109
  223.9 1.2 copy-done.7
  225.1 1.0 copy-done.10
  226.1 0.8 copy-done.15
  227.0 2.1 serving_slots.1
  (58 shorter events, 0.7 us)
Async XLA Ops:
  0.6 0.7 copy-start
  3.9 1.6 copy-start.18
  3.9 2.9 %copy-start.1 = (f32[2,3,2,32,2048]{4,3,2,1,0:T(8,128)S(1)}, f32[2,3,2,32,2048]{4,3,2,1,0:T(8,128)}, u32[]{:S(2)}) copy-start(f32[2,3,2,32,2048]{4,3,2,1,0:T(8,128)} %param.20) | copy-start | bytes 9437188
  5.5 1.4 copy-start.13
  84.4 4.3 %copy-start.3 = (bf16[128,8192]{1,0:T(8,128)(2,1)}, bf16[128,8192]{1,0:T(8,128)(2,1)S(1)}, u32[]{:S(2)}) copy-start(bf16[128,8192]{1,0:T(8,128)(2,1)S(1)} %get-tuple-element.30) | copy-start | bytes 6291460
  84.4 4.6 %copy-start.16 = (bf16[512,2048]{1,0:T(8,128)(2,1)S(1)}, bf16[512,2048]{1,0:T(8,128)(2,1)}, u32[]{:S(2)}) copy-start(bf16[512,2048]{1,0:T(8,128)(2,1)} %param.13) | copy-start | bytes 6291460
  99.7 4.4 %copy-start.20 = (bf16[128,512]{1,0:T(8,128)(2,1)S(1)}, bf16[128,512]{1,0:T(8,128)(2,1)}, u32[]{:S(2)}) copy-start(bf16[128,512]{1,0:T(8,128)(2,1)} %low_sums.1) | copy-start | bytes 393220
  99.7 4.4 %copy-start.17 = (bf16[512,2048]{1,0:T(8,128)(2,1)S(1)}, bf16[512,2048]{1,0:T(8,128)(2,1)}, u32[]{:S(2)}) copy-start(bf16[512,2048]{1,0:T(8,128)(2,1)} %param.13) | copy-start | bytes 6291460
  104.1 0.9 copy-start.19
  104.2 1.6 copy-start.21
  108.4 64.5 %copy-start.4 = (bf16[128,8192]{1,0:T(8,128)(2,1)S(1)}, bf16[128,8192]{1,0:T(8,128)(2,1)}, u32[]{:S(2)}) copy-start(bf16[128,8192]{1,0:T(8,128)(2,1)} %copy-done.3) | copy-start | bytes 6291460
  172.9 1.9 copy-start.5
  172.9 1.9 copy-start.11
  172.9 1.8 copy-start.22
  172.9 1.9 copy-start.23
  175.7 1.2 copy-start.6
  176.9 3.3 %copy-start.2 = (f32[2,3,32,2048]{3,2,1,0:T(8,128)S(1)}, f32[2,3,32,2048]{3,2,1,0:T(8,128)}, u32[]{:S(2)}) copy-start(f32[2,3,32,2048]{3,2,1,0:T(8,128)} %state.2) | copy-start | bytes 4718596
  176.9 3.3 %copy-start.12 = (f32[64,2048]{1,0:T(8,128)S(1)}, f32[64,2048]{1,0:T(8,128)}, u32[]{:S(2)}) copy-start(f32[64,2048]{1,0:T(8,128)} %copy-done.11) | copy-start | bytes 1572868
  180.2 2.6 %copy-start.8 = (bf16[4,64,2048]{2,1,0:T(8,128)(2,1)}, bf16[4,64,2048]{2,1,0:T(8,128)(2,1)S(1)}, u32[]{:S(2)}) copy-start(bf16[4,64,2048]{2,1,0:T(8,128)(2,1)S(1)} %get-tuple-element.43.refs_0_) | copy-start | bytes 3145732
  182.8 0.8 copy-start.9
  184.9 0.6 copy-start.14
  223.9 1.2 copy-start.7
  225.1 1.0 copy-start.10
  226.1 0.8 copy-start.15
